TPU v7x, 512 devices: a whole 4x8x8 slice. The times are simulated.
512 devices in a mesh: seq: 16 (over x, z_lo), res: 32 (over z_hi, y, core).
Axes of the slice: x: 4, y: 8, z: 8 (z_hi: 2, z_lo: 4; z = z_hi * 4 + z_lo), core: 2. Of those that a mesh axis runs over, the one named last changes fastest.
Arguments:
- alignment: bfloat16 [1024, 256, 256], P(('seq', 'res')), may hold values from -6 to 6
- layer_norm_gain: float32 [256], replicated, may hold values from 0.1 to 1.9
- layer_norm_bias: float32 [256], replicated, may hold values from -0.6 to 0.6
- left_projection_weight: bfloat16 [256, 32], replicated, may hold values from -0.375 to 0.375
- left_bias: float32 [32], replicated, may hold values from -0.6 to 0.6
- right_projection_weight: bfloat16 [256, 32], replicated, may hold values from -0.375 to 0.375
- right_bias: float32 [32], replicated, may hold values from -0.6 to 0.6
- out_weight: bfloat16 [1024, 128], replicated, may hold values from -6 to 6
- out_bias: float32 [128], replicated, may hold values from -3 to 3
Outputs:
- pair_update: bfloat16 [256, 256, 128], P('res', 'seq')
All inputs are finite; a program needn't handle non-finite values.
Results may differ from a plain program's by a relative error of at most 0.022.
Values may be sent and summed in bfloat16 or wider, within the bound.
A program may use at most 64 MiB of HBM per device.

v0:
```python
import jax
import jax.numpy as jnp
from jax import lax
from jax.sharding import PartitionSpec as P


def normalize_project(alignment, layer_norm_gain, layer_norm_bias, weight, bias):
    values = alignment.astype(jnp.float32)
    centre = jnp.mean(values, axis=-1, keepdims=True)
    spread = jnp.mean((values - centre) ** 2, axis=-1, keepdims=True)
    normed = (
        (values - centre) * lax.rsqrt(spread + 1e-05) * layer_norm_gain + layer_norm_bias
    ).astype(jnp.bfloat16)
    flat = normed.reshape(-1, normed.shape[-1])
    result = jnp.dot(flat, weight, preferred_element_type=jnp.float32) + bias
    return result.astype(jnp.bfloat16).reshape(normed.shape[:-1] + (weight.shape[1],))


def body(
    alignment,
    layer_norm_gain,
    layer_norm_bias,
    left_projection_weight,
    left_bias,
    right_projection_weight,
    right_bias,
    out_weight,
    out_bias,
):
    res_count = lax.axis_size("res")
    seq_count = lax.axis_size("seq")
    row_count, res_total, chan_count = alignment.shape
    res_block = res_total // res_count
    hidden_width = left_projection_weight.shape[1]
    pair_width = out_weight.shape[1]
    both_weights = jnp.concatenate([left_projection_weight, right_projection_weight], axis=1)
    both_biases = jnp.concatenate([left_bias, right_bias], axis=0)
    arrived = lax.all_to_all(
        alignment.reshape(row_count, res_count, res_block * chan_count),
        "res",
        split_axis=1,
        concat_axis=0,
        tiled=True,
    )
    projected = normalize_project(
        arrived.reshape(row_count * res_count, res_block, chan_count),
        layer_norm_gain,
        layer_norm_bias,
        both_weights,
        both_biases,
    )
    seq_local = projected.shape[0]
    seq_total = seq_local * seq_count
    left_cols = projected[:, :, :hidden_width].reshape(seq_local, res_block * hidden_width)
    right_cols = projected[:, :, hidden_width:].reshape(seq_local, res_block * hidden_width)
    col_piece = lax.all_gather(right_cols, "res", axis=1, tiled=True)
    col_res = col_piece.shape[1] // hidden_width
    outer_block = lax.dot_general(
        left_cols, col_piece, (((0,), (0,)), ((), ())), preferred_element_type=jnp.float32
    ) / float(seq_total)
    outer_block = outer_block.astype(jnp.bfloat16).reshape(
        res_block, hidden_width, col_res, hidden_width
    )
    outer_block = outer_block.transpose(0, 2, 1, 3).reshape(
        res_block * col_res, hidden_width * hidden_width
    )
    term_block = jnp.dot(outer_block, out_weight, preferred_element_type=jnp.float32)
    partial_terms = term_block.reshape(res_block, col_res, pair_width)
    summed = lax.psum_scatter(
        partial_terms.astype(jnp.bfloat16), "seq", scatter_dimension=1, tiled=True
    ).astype(jnp.float32)
    return (summed + out_bias).astype(jnp.bfloat16)


def solution(mesh):
    in_specs = (P(("seq", "res"), None, None), P(), P(), P(), P(), P(), P(), P(), P())
    out_specs = P("res", "seq", None)
    return jax.shard_map(body, mesh=mesh, in_specs=in_specs, out_specs=out_specs, check_vma=False)
```

profile of v0, /device:TPU:8, one launch (start us, length us, event | category | flops | bytes accessed | tf_op | source)
XLA Modules:
  0.0 264.0 jit_solution(11976836676439339691)
XLA Ops:
  6.5 0.0 copy-start
  6.5 0.0 copy-start.2
  6.5 0.0 copy-start.3
  6.5 0.0 copy-start.4
  6.5 0.0 copy-start.5
  6.5 1.1 reshape.64
  7.7 1.0 copy.11
  8.6 16.2 %all-to-all-start = ((bf16[2,32,2048]{2,0,1:T(2,128)(2,1)}), bf16[2,32,2048]{2,0,1:T(2,128)(2,1)S(1)}, u32[]{:S(2)}, u32[]{:S(2)}) async-start(bf16[2,32,2048]{2,0,1:T(2,128)(2,1)} %copy.11), calls=%async_computation | async-start | bytes 524288 | tf_op jit(solution)/shard_map/all_to_all | solution.py:38
  24.8 0.0 all-gather.2.cloned.1.call-start
  24.8 0.7 pad_maximum_fusion
  25.6 15.3 %all-to-all-done = bf16[2,32,2048]{2,0,1:T(2,128)(2,1)S(1)} async-done(((bf16[2,32,2048]{2,0,1:T(2,128)(2,1)}), bf16[2,32,2048]{2,0,1:T(2,128)(2,1)S(1)}, u32[]{:S(2)}, u32[]{:S(2)}) %all-to-all-start) | async-done | bytes 262176 | tf_op jit(solution)/shard_map/all_to_all | solution.py:38
  40.9 0.3 convert_bitcast_fusion
  41.2 0.4 reshape.70
  41.7 0.4 reshape.69
  42.1 0.1 reduce_sum.18
  42.3 0.2 multiply_reduce_fusion
  42.5 0.1 div.15
  42.6 0.1 rsqrt.12
  42.7 0.0 copy-done.2
  42.7 0.0 copy-done.3
  42.7 0.0 copy-done.4
  42.7 0.0 copy-done.5
  42.7 0.3 fusion.1
  43.1 0.1 copy.12
  43.2 0.1 fusion.11
  43.3 0.8 copy.14
  44.1 0.0 all-gather.2.cloned.1.call-update
  44.1 0.0 reduce-scatter.2.cloned.1.call-start
  44.1 0.1 copy.13
  44.3 87.8 %all-gather.2.cloned.1.call-done = bf16[64,8192]{0,1:T(8,128)(2,1)} async-done(((bf16[64,256]{0,1:T(8,128)(2,1)}), bf16[64,8192]{0,1:T(8,128)(2,1)}) %all-gather.2.cloned.1.call-update) | async-done | bytes 1048592 | tf_op jit(solution)/shard_map/all_gather | solution.py:56
  132.1 4.8 %fusion = bf16[256,8192]{1,0:T(8,128)(2,1)} fusion(bf16[64,256]{0,1:T(8,128)(2,1)S(1)} %bitcast.23, bf16[64,8192]{0,1:T(8,128)(2,1)} %all-gather.2.cloned.1.call-done), kind=kOutput, calls=%fused_computation.1 | convolution fusion | flops 272629760 | bytes 5275648 | tf_op jit(solution)/shard_map/dot_general | solution.py:58
  136.8 17.3 %reshape.68 = bf16[8,32,256,32]{3,2,1,0:T(8,128)(2,1)} reshape(bf16[256,8192]{1,0:T(8,128)(2,1)} %fusion) | data formatting | bytes 8388608 | tf_op jit(solution)/shard_map/reshape | solution.py:61
  154.1 14.9 %copy.15 = bf16[8,256,32,32]{1,3,2,0:T(8,128)(2,1)} copy(bf16[8,256,32,32]{3,1,2,0:T(8,128)(2,1)} %bitcast.20) | data formatting | bytes 8388608 | tf_op jit(solution)/shard_map/transpose | solution.py:64
  169.1 0.0 copy-start.1
  169.1 0.0 copy-done
  169.1 4.3 %convolution_convert_fusion = bf16[8,256,128]{2,1,0:T(8,128)(2,1)} fusion(bf16[8,256,1024]{1,2,0:T(8,128)(2,1)} %bitcast.21, bf16[1024,128]{1,0:T(8,128)(2,1)S(1)} %copy-done), kind=kOutput, calls=%fused_computation.2 | convolution fusion | flops 537133056 | bytes 4980736 | tf_op jit(solution)/shard_map/dot_general | solution.py:67
  173.4 0.0 reduce-scatter.2.cloned.1.call-update
  173.4 82.4 %reduce-scatter.2.cloned.1.call-done = bf16[8,16,128]{2,1,0:T(8,128)(2,1)} async-done(((bf16[8,256,128]{2,1,0:T(8,128)(2,1)}), bf16[8,16,128]{2,1,0:T(8,128)(2,1)}) %reduce-scatter.2.cloned.1.call-update) | async-done | bytes 32784 | tf_op jit(solution)/shard_map/reduce_scatter | solution.py:69
  255.8 0.0 copy-done.1
  255.8 1.4 add_convert_fusion.2
  (2 shorter events, 0.0 us)
Async XLA Ops:
  6.5 162.5 %copy-start = (bf16[1024,128]{1,0:T(8,128)(2,1)S(1)}, bf16[1024,128]{1,0:T(8,128)(2,1)}, u32[]{:S(2)}) copy-start(bf16[1024,128]{1,0:T(8,128)(2,1)} %param.16) | copy-start | bytes 786436
  6.5 36.1 %copy-start.2 = (bf16[256,32]{0,1:T(8,128)(2,1)S(1)}, bf16[256,32]{0,1:T(8,128)(2,1)}, u32[]{:S(2)}) copy-start(bf16[256,32]{0,1:T(8,128)(2,1)} %param.14) | copy-start | bytes 49156
  6.5 36.2 %copy-start.3 = (bf16[256,32]{0,1:T(8,128)(2,1)S(1)}, bf16[256,32]{0,1:T(8,128)(2,1)}, u32[]{:S(2)}) copy-start(bf16[256,32]{0,1:T(8,128)(2,1)} %param.12) | copy-start | bytes 49156
  6.5 36.2 %copy-start.4 = (f32[256]{0:T(256)S(1)}, f32[256]{0:T(256)}, u32[]{:S(2)}) copy-start(f32[256]{0:T(256)} %param.11) | copy-start | bytes 3076
  6.5 36.2 %copy-start.5 = (f32[256]{0:T(256)S(1)}, f32[256]{0:T(256)}, u32[]{:S(2)}) copy-start(f32[256]{0:T(256)} %param.10) | copy-start | bytes 3076
  8.6 32.3 %all-to-all-start = ((bf16[2,32,2048]{2,0,1:T(2,128)(2,1)}), bf16[2,32,2048]{2,0,1:T(2,128)(2,1)S(1)}, u32[]{:S(2)}, u32[]{:S(2)}) async-start(bf16[2,32,2048]{2,0,1:T(2,128)(2,1)} %copy.11), calls=%async_computation | async-start | bytes 524288 | tf_op jit(solution)/shard_map/all_to_all | solution.py:38
  24.8 107.3 %all-gather.2.cloned.1.call-start = ((), (), s32[]{:S(2)}) async-start(), calls=%async_computation.2 | async-start | bytes 2162688 | tf_op jit(solution)/shard_map/all_gather | solution.py:56
  44.1 211.7 %reduce-scatter.2.cloned.1.call-start = ((), (), s32[]{:S(2)}) async-start(), calls=%async_computation.3 | async-start | bytes 557056 | tf_op jit(solution)/shard_map/reduce_scatter | solution.py:69
  169.1 86.7 %copy-start.1 = (f32[128]{0:T(128)S(1)}, f32[128]{0:T(128)}, u32[]{:S(2)}) copy-start(f32[128]{0:T(128)} %param.17) | copy-start | bytes 1540
Sparse Core Ops, SparseCore 0:
  44.2 87.7 all-gather.1
  173.5 82.2 reduce-scatter.1
where the time goes:
time: 265 us; the launch traced here: 264 us
  waiting for transfers between devices  186 us (70%)
  local copies, waits for them, and re-layouts  36.5 us (14%)
  starting transfers between devices  16.2 us (6%)
  between operations  13.5 us (5%)
  matrix products  9.43 us (4%)
  other arithmetic  2.79 us (1%)
    all_gather x1, waiting for transfers between devices, body(): col_piece = lax.all_gather(right_cols, 'res', axis=1, tiled=True)  87.8 us
    reduce_scatter x1, waiting for transfers between devices, body(): lax.psum_scatter(partial_terms.astype(jnp.bfloat16), 'seq', scatter_dimen...  82.4 us
    reshape x1, local copies, waits for them, and re-layouts, body(): outer_block.astype(jnp.bfloat16)  17.3 us
    all_to_all x1, starting transfers between devices, body(): lax.all_to_all(alignment.reshape(row_count, res_count, res_block * chan_c...  16.2 us
    all_to_all x1, waiting for transfers between devices, body(): lax.all_to_all(alignment.reshape(row_count, res_count, res_block * chan_c...  15.3 us
    transpose x1, local copies, waits for them, and re-layouts, body(): outer_block.transpose(0, 2, 1, 3)  14.9 us
  transfers between devices with their start and end apart: 3, of which 3 were waited for; matrix products, arithmetic and copies ran while one was open for 0% of the time, Pallas kernels for 0%

commit v1 on v0

v1 whole, which is shorter than its diff:
```python
import functools

import jax
import jax.numpy as jnp
from jax import lax
from jax.experimental import pallas as pl
from jax.experimental.pallas import tpu as pltpu
from jax.sharding import PartitionSpec as P

MESH = pl.DeviceIdType.MESH
F32 = jnp.float32
BF16 = jnp.bfloat16
NX, NY, NZ = 4, 8, 8


def iota(shape, dim):
    return lax.broadcasted_iota(jnp.int32, shape, dim)


def one_hot(condition):
    return jnp.where(condition, 1.0, 0.0).astype(BF16)


def matmul(a, b):
    return jnp.dot(a, b, preferred_element_type=F32)


def contract_rows(a, b):
    return lax.dot_general(a, b, (((0,), (0,)), ((), ())), preferred_element_type=F32)


def device_at(x, y, z, core):
    return (x * 4 + lax.rem(z, 4), lax.div(z, 4) * 16 + y * 2 + core)


def remote(src, dst, sems, k, device):
    return pltpu.make_async_remote_copy(
        src_ref=src,
        dst_ref=dst,
        send_sem=sems[0].at[k],
        recv_sem=sems[1].at[k],
        device_id=device,
        device_id_type=MESH,
    )


def kernel(
    align_hbm, gain_hbm, shift_hbm, wl_hbm, bl_hbm, wr_hbm, br_hbm, ow_hbm, ob_hbm,
    out_ref,
    align, gain, shift, wl, bl, wr, br, ow, ob,
    l_first, r_first, l_z, r_z, l_by_y, r_by_x, l_y, r_all, l_t, t_ref, half_out, half_in, total,
    load_sems, zr_s, zr_r, zl_s, zl_r, xr_s, xr_r, yl_s, yl_r, yr_s, yr_r, xl_s, xl_r, core_s, core_r,
):
    seq, res = lax.axis_index("seq"), lax.axis_index("res")
    x, z_lo = lax.div(seq, 4), lax.rem(seq, 4)
    z_hi, y, core = lax.div(res, 16), lax.rem(lax.div(res, 2), 8), lax.rem(res, 2)
    z = z_hi * 4 + z_lo

    def along_x(k):
        return lax.rem(x + k, NX)

    def along_y(k):
        return lax.rem(y + k, NY)

    def along_z(k):
        return lax.rem(z + k, NZ)

    sibling = device_at(x, y, z, 1 - core)
    x_peer = {k: device_at(along_x(k), y, z, core) for k in range(1, NX)}
    y_peer = {k: device_at(x, along_y(k), z, core) for k in range(1, NY)}
    z_peer = {k: device_at(x, y, along_z(k), core) for k in range(1, NZ)}
    far_first = (4, 3, 5, 2, 6, 1, 7)

    barrier = pltpu.get_barrier_semaphore()
    everyone = [z_peer[k] for k in far_first] + [y_peer[k] for k in far_first]
    everyone += [x_peer[k] for k in (2, 1, 3)] + [sibling]
    for device in everyone:
        pl.semaphore_signal(barrier, inc=1, device_id=device, device_id_type=MESH)

    pairs = (
        (align_hbm, align), (gain_hbm, gain), (shift_hbm, shift), (wl_hbm, wl), (bl_hbm, bl),
        (wr_hbm, wr), (br_hbm, br), (ow_hbm, ow), (ob_hbm, ob),
    )
    loads = [pltpu.make_async_copy(a, b, load_sems.at[n]) for n, (a, b) in enumerate(pairs)]
    for load in loads:
        load.start()
    for load in loads:
        load.wait()

    values = align[...].astype(F32).reshape(512, 256)
    centre = jnp.mean(values, axis=-1, keepdims=True)
    spread = jnp.mean((values - centre) ** 2, axis=-1, keepdims=True)
    normed = ((values - centre) * lax.rsqrt(spread + 1e-05) * gain[...] + shift[...]).astype(BF16)
    repeat = one_hot(jnp.bitwise_and(iota((32, 128), 1), 31) == iota((32, 128), 0))
    weights = jnp.concatenate(
        [contract_rows(w[...], repeat).astype(BF16) for w in (wl, wr)], axis=1
    )
    biases = jnp.concatenate([bl[...]] * 4 + [br[...]] * 4, axis=1)
    projected = matmul(normed, weights) + biases
    lane_group = jnp.bitwise_and(jnp.right_shift(iota((512, 256), 1), 5), 3)
    mine = jnp.bitwise_and(iota((512, 256), 0), 3) == lane_group
    spaced = jnp.where(mine, projected, 0.0).astype(BF16)
    source = iota((128, 512), 1)
    target = jnp.bitwise_and(jnp.right_shift(source, 2), 63) * 2 + jnp.right_shift(source, 8)
    gathered = matmul(one_hot(target == iota((128, 512), 0)), spaced)
    l_first[...] = gathered[:, :128].astype(BF16).reshape(2, 64, 128)
    by_x = gathered[:, 128:]
    for b in range(4):
        r_first[b] = jnp.concatenate(
            [by_x[a * 32 + b * 8 : a * 32 + b * 8 + 8] for a in range(4)], axis=0
        ).astype(BF16)
    l_z[z] = l_first[z_hi]
    r_z[z] = r_first[z_lo]

    pl.semaphore_wait(barrier, len(everyone))

    zr, zl = [], []
    for k in far_first:
        to = along_z(k)
        copy = remote(r_first.at[lax.rem(to, 4)], r_z.at[z], (zr_s, zr_r), k - 1, z_peer[k])
        copy.start()
        zr.append(copy)
    for k in far_first:
        to = along_z(k)
        copy = remote(l_first.at[lax.div(to, 4)], l_z.at[z], (zl_s, zl_r), k - 1, z_peer[k])
        copy.start()
        zl.append(copy)

    o, n = iota((256, 256), 0), iota((256, 256), 1)
    o_vh, o_z, o_s = jnp.right_shift(o, 4), jnp.bitwise_and(jnp.right_shift(o, 1), 7), jnp.bitwise_and(o, 1)
    regroup = one_hot(n == o_z * 32 + o_vh * 2 + o_s)
    o, n = iota((512, 512), 0), iota((512, 512), 1)
    turn = one_hot(n == jnp.bitwise_and(o, 15) * 32 + jnp.right_shift(o, 4))

    for copy in zr:
        copy.wait_recv()
    moved = matmul(regroup, r_z[...].reshape(256, 128)).astype(BF16)
    for v in range(4):
        for h in range(4):
            r_by_x[v, :, h * 128 : (h + 1) * 128] = moved[v * 64 + h * 16 : v * 64 + h * 16 + 16]
    r_all[y, x] = r_by_x[x]
    xr = []
    for k in (2, 1, 3):
        copy = remote(r_by_x.at[along_x(k)], r_all.at[y, x], (xr_s, xr_r), k - 1, x_peer[k])
        copy.start()
        xr.append(copy)

    for copy in zl:
        copy.wait_recv()
    for part in range(2):
        moved = matmul(regroup, l_z[:, part * 32 : part * 32 + 32, :].reshape(256, 128)).astype(BF16)
        for v in range(4):
            for h in range(4):
                l_by_y[part * 4 + v, :, h * 128 : (h + 1) * 128] = moved[
                    v * 64 + h * 16 : v * 64 + h * 16 + 16
                ]
    l_y[y] = l_by_y[y]
    yl = []
    for k in far_first:
        copy = remote(l_by_y.at[along_y(k)], l_y.at[y], (yl_s, yl_r), k - 1, y_peer[k])
        copy.start()
        yl.append(copy)

    for copy in xr:
        copy.wait_recv()
    yr = []
    for k in far_first:
        copy = remote(r_all.at[y], r_all.at[y], (yr_s, yr_r), k - 1, y_peer[k])
        copy.start()
        yr.append(copy)

    for copy in yl:
        copy.wait_recv()
    l_t[x] = lax.dot_general(
        turn, l_y[...].reshape(128, 512), (((1,), (1,)), ((), ())), preferred_element_type=F32
    ).astype(BF16)
    xl = []
    for k in (2, 1, 3):
        copy = remote(l_t.at[x], l_t.at[x], (xl_s, xl_r), k - 1, x_peer[k])
        copy.start()
        xl.append(copy)

    for copy in xl + yr:
        copy.wait_recv()
    left = jnp.concatenate([l_t[a] for a in range(NX)], axis=1)
    right = jnp.concatenate([r_all[b, a] for a in range(NX) for b in range(NY)], axis=0)
    outer = (matmul(left, right) * (1.0 / 1024)).astype(BF16)
    lane = iota((128, 128), 1)
    low, even = lane < 64, jnp.bitwise_and(lane, 32) == 0
    blocks = outer.reshape(8, 4, 16, 512)
    for h in range(4):
        a, b, c, d = (
            blocks[:, n, :, h * 128 : (h + 1) * 128].reshape(128, 128).astype(F32) for n in range(4)
        )
        a, c = jnp.where(low, a, pltpu.roll(c, 64, 1)), jnp.where(low, pltpu.roll(a, 64, 1), c)
        b, d = jnp.where(low, b, pltpu.roll(d, 64, 1)), jnp.where(low, pltpu.roll(b, 64, 1), d)
        a, b = jnp.where(even, a, pltpu.roll(b, 32, 1)), jnp.where(even, pltpu.roll(a, 96, 1), b)
        c, d = jnp.where(even, c, pltpu.roll(d, 32, 1)), jnp.where(even, pltpu.roll(c, 96, 1), d)
        for n, block in enumerate((a, b, c, d)):
            block = block.astype(BF16)
            row = (h * 4 + n) * 16
            for m in range(8):
                t_ref[row : row + 16, m * 128 : (m + 1) * 128] = block[m * 16 : m * 16 + 16]
    term = matmul(t_ref[...], ow[...]).reshape(16, 2, 8, 128)
    half_out[...] = jnp.where(core == 0, term[:, 1], term[:, 0]).reshape(128, 128)
    swap = remote(half_out, half_in, (core_s, core_r), 0, sibling)
    swap.start()
    kept = jnp.where(core == 0, term[:, 0], term[:, 1]).reshape(128, 128)
    swap.wait_recv()
    total[...] = kept + half_in[...]
    for i in range(8):
        out_ref[i] = (total[pl.ds(i, 16, stride=8), :] + ob[...]).astype(BF16)
    for copy in zr + zl + xr + yl + yr + xl + [swap]:
        copy.wait_send()


def body(alignment, gain, shift, wl, bl, wr, br, ow, ob):
    any_space = pl.BlockSpec(memory_space=pl.ANY)
    dma = pltpu.SemaphoreType.DMA
    args = (
        alignment, gain.reshape(1, -1), shift.reshape(1, -1), wl.T, bl.reshape(1, -1),
        wr.T, br.reshape(1, -1), ow, ob.reshape(1, -1),
    )
    scratch = [pltpu.VMEM(a.shape, a.dtype) for a in args]
    scratch += [
        pltpu.VMEM((2, 64, 128), BF16),
        pltpu.VMEM((4, 32, 128), BF16),
        pltpu.VMEM((8, 64, 128), BF16),
        pltpu.VMEM((8, 32, 128), BF16),
        pltpu.VMEM((8, 16, 512), BF16),
        pltpu.VMEM((4, 16, 512), BF16),
        pltpu.VMEM((8, 16, 512), BF16),
        pltpu.VMEM((8, 4, 16, 512), BF16),
        pltpu.VMEM((4, 512, 128), BF16),
        pltpu.VMEM((256, 1024), BF16),
        pltpu.VMEM((128, 128), F32),
        pltpu.VMEM((128, 128), F32),
        pltpu.VMEM((128, 128), F32),
        dma((len(args),)),
    ]
    for n in (7, 7, 3, 7, 7, 3, 1):
        scratch += [dma((n,)), dma((n,))]
    return pl.pallas_call(
        kernel,
        out_shape=jax.ShapeDtypeStruct((8, 16, 128), BF16),
        in_specs=[any_space] * len(args),
        out_specs=pl.BlockSpec(memory_space=pltpu.VMEM),
        scratch_shapes=scratch,
        compiler_params=pltpu.CompilerParams(
            collective_id=0, has_side_effects=True, vmem_limit_bytes=62 << 20
        ),
    )(*args)


def solution(mesh):
    in_specs = (P(("seq", "res"), None, None), P(), P(), P(), P(), P(), P(), P(), P())
    return jax.shard_map(
        body, mesh=mesh, in_specs=in_specs, out_specs=P("res", "seq", None), check_vma=False
    )
```

time: 265 us -> 42.2 us (0.16)
  the two profiles are of different devices: /device:TPU:8 before, /device:TPU:1 now
where the time goes in v1:
time: 42.2 us; the launch traced here: 42 us
  Pallas kernels  40.6 us (96%)
  local copies, waits for them, and re-layouts  1.38 us (3%)
    pallas_call x1, Pallas kernels, body(): pl.pallas_call(kernel, out_shape=jax.ShapeDtypeStruct((8, 16, 128), BF16)...  40.6 us
    unnamed x1, local copies, waits for them, and re-layouts  1.38 us

profile of v1, /device:TPU:1, one launch (start us, length us, event | category | flops | bytes accessed | tf_op | source)
XLA Modules:
  0.0 42.0 jit_solution(6269079304861919868)
XLA Ops:
  0.0 40.6 %shard_map.91 = bf16[8,16,128]{2,1,0:T(8,128)(2,1)} custom-call(bf16[2,256,256]{2,1,0:T(8,128)(2,1)} %align_hbm.1, f32[1,256]{1,0:T(1,128)} %bitcast.9, f32[1,256]{1,0:T(1,128)} %bitcast.10, bf16[32,256]{1,0:T(8,128)(2,1)} %bitcast.7, f32[1,32]{1,0:T(1,128)} %bitcast.11, bf16[32,256]{1,0:T(8,128)(2,1)} %bitcast.8, f32[1,32]{1,0:T(1,128)} %bitcast.12, ...), custom_call_target="tpu_custom_call" | custom-call | tf_op jit(solution)/shard_map/pallas_call | solution.py:243
  40.6 1.4 %copy.11 = bf16[8,16,128]{2,1,0:T(8,128)(2,1)} copy(bf16[8,16,128]{2,1,0:T(8,128)(2,1)} %shard_map.91) | data formatting | bytes 65536

commit v2 on v1

--- a/solution.py
+++ b/solution.py
@@ -48,7 +48,7 @@
     align_hbm, gain_hbm, shift_hbm, wl_hbm, bl_hbm, wr_hbm, br_hbm, ow_hbm, ob_hbm,
     out_ref,
     align, gain, shift, wl, bl, wr, br, ow, ob,
-    l_first, r_first, l_z, r_z, l_by_y, r_by_x, l_y, r_all, l_t, t_ref, half_out, half_in, total,
+    l_first, r_first, l_y, r_z, l_by_z, r_by_x, l_z, r_all, l_t, t_ref, half_out, half_in, total,
     load_sems, zr_s, zr_r, zl_s, zl_r, xr_s, xr_r, yl_s, yl_r, yr_s, yr_r, xl_s, xl_r, core_s, core_r,
 ):
     seq, res = lax.axis_index("seq"), lax.axis_index("res")
@@ -103,32 +103,37 @@
     source = iota((128, 512), 1)
     target = jnp.bitwise_and(jnp.right_shift(source, 2), 63) * 2 + jnp.right_shift(source, 8)
     gathered = matmul(one_hot(target == iota((128, 512), 0)), spaced)
-    l_first[...] = gathered[:, :128].astype(BF16).reshape(2, 64, 128)
+    for b in range(NY):
+        l_first[b] = jnp.concatenate(
+            [gathered[a * 64 + b * 8 : a * 64 + b * 8 + 8, :128] for a in range(2)], axis=0
+        ).astype(BF16)
     by_x = gathered[:, 128:]
     for b in range(4):
         r_first[b] = jnp.concatenate(
             [by_x[a * 32 + b * 8 : a * 32 + b * 8 + 8] for a in range(4)], axis=0
         ).astype(BF16)
-    l_z[z] = l_first[z_hi]
+    l_y[y] = l_first[y]
     r_z[z] = r_first[z_lo]
 
     pl.semaphore_wait(barrier, len(everyone))
 
-    zr, zl = [], []
+    zr, yl = [], []
     for k in far_first:
         to = along_z(k)
         copy = remote(r_first.at[lax.rem(to, 4)], r_z.at[z], (zr_s, zr_r), k - 1, z_peer[k])
         copy.start()
         zr.append(copy)
     for k in far_first:
-        to = along_z(k)
-        copy = remote(l_first.at[lax.div(to, 4)], l_z.at[z], (zl_s, zl_r), k - 1, z_peer[k])
-        copy.start()
-        zl.append(copy)
+        copy = remote(l_first.at[along_y(k)], l_y.at[y], (yl_s, yl_r), k - 1, y_peer[k])
+        copy.start()
+        yl.append(copy)
 
     o, n = iota((256, 256), 0), iota((256, 256), 1)
     o_vh, o_z, o_s = jnp.right_shift(o, 4), jnp.bitwise_and(jnp.right_shift(o, 1), 7), jnp.bitwise_and(o, 1)
     regroup = one_hot(n == o_z * 32 + o_vh * 2 + o_s)
+    o, n = iota((128, 128), 0), iota((128, 128), 1)
+    o_zh, o_y, o_s = jnp.right_shift(o, 4), jnp.bitwise_and(jnp.right_shift(o, 1), 7), jnp.bitwise_and(o, 1)
+    regroup_l = one_hot(n == o_y * 16 + o_zh * 2 + o_s)
     o, n = iota((512, 512), 0), iota((512, 512), 1)
     turn = one_hot(n == jnp.bitwise_and(o, 15) * 32 + jnp.right_shift(o, 4))
 
@@ -145,34 +150,33 @@
         copy.start()
         xr.append(copy)
 
+    for copy in yl:
+        copy.wait_recv()
+    moved = matmul(regroup_l, l_y[...].reshape(128, 128)).astype(BF16)
+    for v in range(2):
+        for h in range(4):
+            l_by_z[v, :, h * 128 : (h + 1) * 128] = moved[v * 64 + h * 16 : v * 64 + h * 16 + 16]
+    l_z[z] = l_by_z[z_hi]
+    zl = []
+    for k in far_first:
+        to = along_z(k)
+        copy = remote(l_by_z.at[lax.div(to, 4)], l_z.at[z], (zl_s, zl_r), k - 1, z_peer[k])
+        copy.start()
+        zl.append(copy)
+
+    for copy in xr:
+        copy.wait_recv()
+    yr = []
+    for k in far_first:
+        copy = remote(r_all.at[y], r_all.at[y], (yr_s, yr_r), k - 1, y_peer[k])
+        copy.start()
+        yr.append(copy)
+
     for copy in zl:
         copy.wait_recv()
-    for part in range(2):
-        moved = matmul(regroup, l_z[:, part * 32 : part * 32 + 32, :].reshape(256, 128)).astype(BF16)
-        for v in range(4):
-            for h in range(4):
-                l_by_y[part * 4 + v, :, h * 128 : (h + 1) * 128] = moved[
-                    v * 64 + h * 16 : v * 64 + h * 16 + 16
-                ]
-    l_y[y] = l_by_y[y]
-    yl = []
-    for k in far_first:
-        copy = remote(l_by_y.at[along_y(k)], l_y.at[y], (yl_s, yl_r), k - 1, y_peer[k])
-        copy.start()
-        yl.append(copy)
-
-    for copy in xr:
-        copy.wait_recv()
-    yr = []
-    for k in far_first:
-        copy = remote(r_all.at[y], r_all.at[y], (yr_s, yr_r), k - 1, y_peer[k])
-        copy.start()
-        yr.append(copy)
-
-    for copy in yl:
-        copy.wait_recv()
+    ordered = matmul(regroup_l, l_z[...].reshape(128, 512)).astype(BF16)
     l_t[x] = lax.dot_general(
-        turn, l_y[...].reshape(128, 512), (((1,), (1,)), ((), ())), preferred_element_type=F32
+        turn, ordered, (((1,), (1,)), ((), ())), preferred_element_type=F32
     ).astype(BF16)
     xl = []
     for k in (2, 1, 3):
@@ -223,11 +227,11 @@
     )
     scratch = [pltpu.VMEM(a.shape, a.dtype) for a in args]
     scratch += [
-        pltpu.VMEM((2, 64, 128), BF16),
+        pltpu.VMEM((8, 16, 128), BF16),
         pltpu.VMEM((4, 32, 128), BF16),
-        pltpu.VMEM((8, 64, 128), BF16),
+        pltpu.VMEM((8, 16, 128), BF16),
         pltpu.VMEM((8, 32, 128), BF16),
-        pltpu.VMEM((8, 16, 512), BF16),
+        pltpu.VMEM((2, 16, 512), BF16),
         pltpu.VMEM((4, 16, 512), BF16),
         pltpu.VMEM((8, 16, 512), BF16),
         pltpu.VMEM((8, 4, 16, 512), BF16),
@@ -240,6 +244,7 @@
     ]
     for n in (7, 7, 3, 7, 7, 3, 1):
         scratch += [dma((n,)), dma((n,))]
+    args = tuple(pltpu.with_memory_space_constraint(a, pltpu.HBM) for a in args)
     return pl.pallas_call(
         kernel,
         out_shape=jax.ShapeDtypeStruct((8, 16, 128), BF16),
@@ -247,7 +252,7 @@
         out_specs=pl.BlockSpec(memory_space=pltpu.VMEM),
         scratch_shapes=scratch,
         compiler_params=pltpu.CompilerParams(
-            collective_id=0, has_side_effects=True, vmem_limit_bytes=62 << 20
+            collective_id=0, has_side_effects=True, vmem_limit_bytes=32 << 20
         ),
     )(*args)
 

time: 42.2 us -> 38.7 us (0.917)
  Pallas kernels: 40.6 us -> 37.9 us
  local copies, waits for them, and re-layouts: 1.38 us -> 0.62 us
    pallas_call x1, Pallas kernels: 40.6 us -> 37.9 us  [body(): pl.pallas_call(kernel, out_shape=jax.ShapeDtypeStruct((8, 16, 128), BF16)...]
    unnamed x1, local copies, waits for them, and re-layouts: 1.38 us -> 0.62 us
where the time goes in v2:
time: 38.7 us; the launch traced here: 38.5 us
  Pallas kernels  37.9 us (98%)
  local copies, waits for them, and re-layouts  0.62 us (2%)
    pallas_call x1, Pallas kernels, body(): pl.pallas_call(kernel, out_shape=jax.ShapeDtypeStruct((8, 16, 128), BF16)...  37.9 us

profile of v2, /device:TPU:1, one launch (start us, length us, event | category | flops | bytes accessed | tf_op | source)
XLA Modules:
  0.0 38.5 jit_solution(10207029599996528027)
XLA Ops:
  0.0 37.9 %shard_map.91 = bf16[8,16,128]{2,1,0:T(8,128)(2,1)S(1)} custom-call(bf16[2,256,256]{2,1,0:T(8,128)(2,1)} %align_hbm.1, f32[1,256]{1,0:T(1,128)} %bitcast.9, f32[1,256]{1,0:T(1,128)} %bitcast.10, bf16[32,256]{1,0:T(8,128)(2,1)} %bitcast.7, f32[1,32]{1,0:T(1,128)} %bitcast.11, bf16[32,256]{1,0:T(8,128)(2,1)} %bitcast.8, f32[1,32]{1,0:T(1,128)} %bitcast.12, ...), custom_call_target="tpu_custom_call" | custom-call | tf_op jit(solution)/shard_map/pallas_call | solution.py:248
  37.9 0.6 %copy.11 = bf16[8,16,128]{2,1,0:T(8,128)(2,1)} copy(bf16[8,16,128]{2,1,0:T(8,128)(2,1)S(1)} %shard_map.91) | data formatting | bytes 65536

commit v3 on v2

--- a/solution.py
+++ b/solution.py
@@ -48,8 +48,9 @@
     align_hbm, gain_hbm, shift_hbm, wl_hbm, bl_hbm, wr_hbm, br_hbm, ow_hbm, ob_hbm,
     out_ref,
     align, gain, shift, wl, bl, wr, br, ow, ob,
-    l_first, r_first, l_y, r_z, l_by_z, r_by_x, l_z, r_all, l_t, t_ref, half_out, half_in, total,
-    load_sems, zr_s, zr_r, zl_s, zl_r, xr_s, xr_r, yl_s, yl_r, yr_s, yr_r, xl_s, xl_r, core_s, core_r,
+    l_first, ra_first, rb_first, l_y, ra_z, rb_y, l_by_z, ra_by_x, rb_by_x, l_z, ra_all, rb_x, rb_all, l_t, t_ref, half_out, half_in, total,
+    load_sems, za_s, za_r, zl_s, zl_r, xa_s, xa_r, yl_s, yl_r, ya_s, ya_r, xl_s, xl_r, yb_s, yb_r, xb_s, xb_r,
+    zb_s, zb_r, core_s, core_r,
 ):
     seq, res = lax.axis_index("seq"), lax.axis_index("res")
     x, z_lo = lax.div(seq, 4), lax.rem(seq, 4)
@@ -100,94 +101,102 @@
     lane_group = jnp.bitwise_and(jnp.right_shift(iota((512, 256), 1), 5), 3)
     mine = jnp.bitwise_and(iota((512, 256), 0), 3) == lane_group
     spaced = jnp.where(mine, projected, 0.0).astype(BF16)
-    source = iota((128, 512), 1)
-    target = jnp.bitwise_and(jnp.right_shift(source, 2), 63) * 2 + jnp.right_shift(source, 8)
-    gathered = matmul(one_hot(target == iota((128, 512), 0)), spaced)
-    for b in range(NY):
-        l_first[b] = jnp.concatenate(
-            [gathered[a * 64 + b * 8 : a * 64 + b * 8 + 8, :128] for a in range(2)], axis=0
-        ).astype(BF16)
-    by_x = gathered[:, 128:]
-    for b in range(4):
-        r_first[b] = jnp.concatenate(
-            [by_x[a * 32 + b * 8 : a * 32 + b * 8 + 8] for a in range(4)], axis=0
-        ).astype(BF16)
+    o, n = iota((128, 512), 0), iota((128, 512), 1)
+    n_s, n_h = jnp.right_shift(n, 8), jnp.bitwise_and(jnp.right_shift(n, 2), 3)
+    n_y, n_zh = jnp.bitwise_and(jnp.right_shift(n, 4), 7), jnp.bitwise_and(jnp.right_shift(n, 7), 1)
+    pick_l = one_hot(o == n_y * 16 + n_zh * 8 + n_h * 2 + n_s)
+    n_zl, n_x = jnp.bitwise_and(jnp.right_shift(n, 4), 3), jnp.bitwise_and(jnp.right_shift(n, 6), 3)
+    row_a = n_zl * 16 + n_x * 4 + n_h * 2 + n_s
+    row_b = 64 + n_x * 16 + n_zl * 4 + (n_h - 2) * 2 + n_s
+    pick_r = one_hot(o == jnp.where(n_h < 2, row_a, row_b))
+    l_first[...] = matmul(pick_l, spaced[:, :128]).astype(BF16).reshape(8, 16, 128)
+    picked = matmul(pick_r, spaced[:, 128:]).astype(BF16)
+    ra_first[...] = picked[:64].reshape(4, 16, 128)
+    rb_first[...] = picked[64:]
     l_y[y] = l_first[y]
-    r_z[z] = r_first[z_lo]
+    ra_z[z] = ra_first[z_lo]
+    rb_y[y] = rb_first[...]
 
     pl.semaphore_wait(barrier, len(everyone))
 
-    zr, yl = [], []
-    for k in far_first:
-        to = along_z(k)
-        copy = remote(r_first.at[lax.rem(to, 4)], r_z.at[z], (zr_s, zr_r), k - 1, z_peer[k])
-        copy.start()
-        zr.append(copy)
-    for k in far_first:
-        copy = remote(l_first.at[along_y(k)], l_y.at[y], (yl_s, yl_r), k - 1, y_peer[k])
-        copy.start()
-        yl.append(copy)
-
-    o, n = iota((256, 256), 0), iota((256, 256), 1)
-    o_vh, o_z, o_s = jnp.right_shift(o, 4), jnp.bitwise_and(jnp.right_shift(o, 1), 7), jnp.bitwise_and(o, 1)
-    regroup = one_hot(n == o_z * 32 + o_vh * 2 + o_s)
+    def to_all(peers, order, sems, src, dst):
+        copies = []
+        for k in order:
+            copy = remote(src(k), dst, sems, k - 1, peers[k])
+            copy.start()
+            copies.append(copy)
+        return copies
+
+    def arrive(copies):
+        for copy in copies:
+            copy.wait_recv()
+
+    x_order = (2, 1, 3)
+    za = to_all(z_peer, far_first, (za_s, za_r), lambda k: ra_first.at[lax.rem(along_z(k), 4)], ra_z.at[z])
+    yl = to_all(y_peer, far_first, (yl_s, yl_r), lambda k: l_first.at[along_y(k)], l_y.at[y])
+    yb = to_all(y_peer, far_first, (yb_s, yb_r), lambda k: rb_first, rb_y.at[y])
+
     o, n = iota((128, 128), 0), iota((128, 128), 1)
-    o_zh, o_y, o_s = jnp.right_shift(o, 4), jnp.bitwise_and(jnp.right_shift(o, 1), 7), jnp.bitwise_and(o, 1)
-    regroup_l = one_hot(n == o_y * 16 + o_zh * 2 + o_s)
+    o_v, o_m, o_s = jnp.right_shift(o, 4), jnp.bitwise_and(jnp.right_shift(o, 1), 7), jnp.bitwise_and(o, 1)
+    regroup = one_hot(n == o_m * 16 + o_v * 2 + o_s)
     o, n = iota((512, 512), 0), iota((512, 512), 1)
     turn = one_hot(n == jnp.bitwise_and(o, 15) * 32 + jnp.right_shift(o, 4))
 
-    for copy in zr:
-        copy.wait_recv()
-    moved = matmul(regroup, r_z[...].reshape(256, 128)).astype(BF16)
+    arrive(za)
+    moved = matmul(regroup, ra_z[...].reshape(128, 128)).astype(BF16)
     for v in range(4):
-        for h in range(4):
-            r_by_x[v, :, h * 128 : (h + 1) * 128] = moved[v * 64 + h * 16 : v * 64 + h * 16 + 16]
-    r_all[y, x] = r_by_x[x]
-    xr = []
-    for k in (2, 1, 3):
-        copy = remote(r_by_x.at[along_x(k)], r_all.at[y, x], (xr_s, xr_r), k - 1, x_peer[k])
-        copy.start()
-        xr.append(copy)
-
-    for copy in yl:
-        copy.wait_recv()
-    moved = matmul(regroup_l, l_y[...].reshape(128, 128)).astype(BF16)
+        for h in range(2):
+            ra_by_x[v, :, h * 128 : (h + 1) * 128] = moved[v * 32 + h * 16 : v * 32 + h * 16 + 16]
+    ra_all[y, x] = ra_by_x[x]
+    xa = to_all(x_peer, x_order, (xa_s, xa_r), lambda k: ra_by_x.at[along_x(k)], ra_all.at[y, x])
+
+    arrive(yl)
+    moved = matmul(regroup, l_y[...].reshape(128, 128)).astype(BF16)
     for v in range(2):
         for h in range(4):
             l_by_z[v, :, h * 128 : (h + 1) * 128] = moved[v * 64 + h * 16 : v * 64 + h * 16 + 16]
     l_z[z] = l_by_z[z_hi]
-    zl = []
-    for k in far_first:
-        to = along_z(k)
-        copy = remote(l_by_z.at[lax.div(to, 4)], l_z.at[z], (zl_s, zl_r), k - 1, z_peer[k])
-        copy.start()
-        zl.append(copy)
-
-    for copy in xr:
-        copy.wait_recv()
-    yr = []
-    for k in far_first:
-        copy = remote(r_all.at[y], r_all.at[y], (yr_s, yr_r), k - 1, y_peer[k])
-        copy.start()
-        yr.append(copy)
-
-    for copy in zl:
-        copy.wait_recv()
-    ordered = matmul(regroup_l, l_z[...].reshape(128, 512)).astype(BF16)
+    zl = to_all(z_peer, far_first, (zl_s, zl_r), lambda k: l_by_z.at[lax.div(along_z(k), 4)], l_z.at[z])
+
+    arrive(yb)
+    wide = jnp.concatenate(
+        [rb_y[:, a * 16 : a * 16 + 16, :].reshape(128, 128) for a in range(NX)], axis=1
+    )
+    moved = matmul(regroup, wide).astype(BF16)
+    for a in range(NX):
+        for v in range(4):
+            for h in range(2):
+                rb_by_x[a, v, :, h * 128 : (h + 1) * 128] = moved[
+                    v * 32 + h * 16 : v * 32 + h * 16 + 16, a * 128 : (a + 1) * 128
+                ]
+    rb_x[:, x] = rb_by_x[x]
+    xb = to_all(x_peer, x_order, (xb_s, xb_r), lambda k: rb_by_x.at[along_x(k)], rb_x.at[:, x])
+
+    arrive(xa)
+    ya = to_all(y_peer, far_first, (ya_s, ya_r), lambda k: ra_all.at[y], ra_all.at[y])
+
+    arrive(xb)
+    rb_all[z] = rb_x[z_lo]
+    zb = to_all(z_peer, far_first, (zb_s, zb_r), lambda k: rb_x.at[lax.rem(along_z(k), 4)], rb_all.at[z])
+
+    arrive(zl)
     l_t[x] = lax.dot_general(
-        turn, ordered, (((1,), (1,)), ((), ())), preferred_element_type=F32
+        turn, l_z[...].reshape(128, 512), (((1,), (1,)), ((), ())), preferred_element_type=F32
     ).astype(BF16)
-    xl = []
-    for k in (2, 1, 3):
-        copy = remote(l_t.at[x], l_t.at[x], (xl_s, xl_r), k - 1, x_peer[k])
-        copy.start()
-        xl.append(copy)
-
-    for copy in xl + yr:
-        copy.wait_recv()
+    xl = to_all(x_peer, x_order, (xl_s, xl_r), lambda k: l_t.at[x], l_t.at[x])
+
+    arrive(ya)
+    right_a = [
+        matmul(regroup, jnp.concatenate([ra_all[b, a] for b in range(NY)], axis=0)).astype(BF16)
+        for a in range(NX)
+    ]
+    arrive(zb)
+    right_b = [rb_all[b, a] for a in range(NX) for b in range(NZ)]
+    right = jnp.concatenate(
+        [jnp.concatenate(right_a, axis=0), jnp.concatenate(right_b, axis=0)], axis=1
+    )
+    arrive(xl)
     left = jnp.concatenate([l_t[a] for a in range(NX)], axis=1)
-    right = jnp.concatenate([r_all[b, a] for a in range(NX) for b in range(NY)], axis=0)
     outer = (matmul(left, right) * (1.0 / 1024)).astype(BF16)
     lane = iota((128, 128), 1)
     low, even = lane < 64, jnp.bitwise_and(lane, 32) == 0
@@ -210,11 +219,11 @@
     swap = remote(half_out, half_in, (core_s, core_r), 0, sibling)
     swap.start()
     kept = jnp.where(core == 0, term[:, 0], term[:, 1]).reshape(128, 128)
-    swap.wait_recv()
+    arrive([swap])
     total[...] = kept + half_in[...]
     for i in range(8):
         out_ref[i] = (total[pl.ds(i, 16, stride=8), :] + ob[...]).astype(BF16)
-    for copy in zr + zl + xr + yl + yr + xl + [swap]:
+    for copy in za + yl + yb + xa + zl + xb + ya + zb + xl + [swap]:
         copy.wait_send()
 
 
@@ -228,13 +237,18 @@
     scratch = [pltpu.VMEM(a.shape, a.dtype) for a in args]
     scratch += [
         pltpu.VMEM((8, 16, 128), BF16),
-        pltpu.VMEM((4, 32, 128), BF16),
+        pltpu.VMEM((4, 16, 128), BF16),
+        pltpu.VMEM((64, 128), BF16),
         pltpu.VMEM((8, 16, 128), BF16),
-        pltpu.VMEM((8, 32, 128), BF16),
+        pltpu.VMEM((8, 16, 128), BF16),
+        pltpu.VMEM((8, 64, 128), BF16),
         pltpu.VMEM((2, 16, 512), BF16),
-        pltpu.VMEM((4, 16, 512), BF16),
+        pltpu.VMEM((4, 16, 256), BF16),
+        pltpu.VMEM((4, 4, 16, 256), BF16),
         pltpu.VMEM((8, 16, 512), BF16),
-        pltpu.VMEM((8, 4, 16, 512), BF16),
+        pltpu.VMEM((8, 4, 16, 256), BF16),
+        pltpu.VMEM((4, 4, 16, 256), BF16),
+        pltpu.VMEM((8, 4, 16, 256), BF16),
         pltpu.VMEM((4, 512, 128), BF16),
         pltpu.VMEM((256, 1024), BF16),
         pltpu.VMEM((128, 128), F32),
@@ -242,7 +256,7 @@
         pltpu.VMEM((128, 128), F32),
         dma((len(args),)),
     ]
-    for n in (7, 7, 3, 7, 7, 3, 1):
+    for n in (7, 7, 3, 7, 7, 3, 7, 3, 7, 1):
         scratch += [dma((n,)), dma((n,))]
     args = tuple(pltpu.with_memory_space_constraint(a, pltpu.HBM) for a in args)
     return pl.pallas_call(

time: 38.7 us -> 36.1 us (0.933)
  Pallas kernels: 37.9 us -> 35.3 us
    pallas_call x1, Pallas kernels: 37.9 us -> 35.3 us  [body(): pl.pallas_call(kernel, out_shape=jax.ShapeDtypeStruct((8, 16, 128), BF16)...]
where the time goes in v3:
time: 36.1 us; the launch traced here: 36 us
  Pallas kernels  35.3 us (98%)
  local copies, waits for them, and re-layouts  0.62 us (2%)
    pallas_call x1, Pallas kernels, body(): pl.pallas_call(kernel, out_shape=jax.ShapeDtypeStruct((8, 16, 128), BF16)...  35.3 us

profile of v3, /device:TPU:1, one launch (start us, length us, event | category | flops | bytes accessed | tf_op | source)
XLA Modules:
  0.0 36.0 jit_solution(2797876905068997031)
XLA Ops:
  0.0 35.3 %shard_map.91 = bf16[8,16,128]{2,1,0:T(8,128)(2,1)S(1)} custom-call(bf16[2,256,256]{2,1,0:T(8,128)(2,1)} %align_hbm.1, f32[1,256]{1,0:T(1,128)} %bitcast.9, f32[1,256]{1,0:T(1,128)} %bitcast.10, bf16[32,256]{1,0:T(8,128)(2,1)} %bitcast.7, f32[1,32]{1,0:T(1,128)} %bitcast.11, bf16[32,256]{1,0:T(8,128)(2,1)} %bitcast.8, f32[1,32]{1,0:T(1,128)} %bitcast.12, ...), custom_call_target="tpu_custom_call" | custom-call | tf_op jit(solution)/shard_map/pallas_call | solution.py:262
  35.4 0.6 %copy.11 = bf16[8,16,128]{2,1,0:T(8,128)(2,1)} copy(bf16[8,16,128]{2,1,0:T(8,128)(2,1)S(1)} %shard_map.91) | data formatting | bytes 65536

commit v4 on v3

--- a/solution.py
+++ b/solution.py
@@ -48,8 +48,8 @@
     align_hbm, gain_hbm, shift_hbm, wl_hbm, bl_hbm, wr_hbm, br_hbm, ow_hbm, ob_hbm,
     out_ref,
     align, gain, shift, wl, bl, wr, br, ow, ob,
-    l_first, ra_first, rb_first, l_y, ra_z, rb_y, l_by_z, ra_by_x, rb_by_x, l_z, ra_all, rb_x, rb_all, l_t, t_ref, half_out, half_in, total,
-    load_sems, za_s, za_r, zl_s, zl_r, xa_s, xa_r, yl_s, yl_r, ya_s, ya_r, xl_s, xl_r, yb_s, yb_r, xb_s, xb_r,
+    l_first, ra_first, rb_first, l_y, ra_z, rb_y, l_by_z, ra_by_x, rb_by_x, l_all, ra_all, rb_x, rb_all, t_ref, half_out, half_in, total,
+    load_sems, za_s, za_r, near_s, near_r, far_s, far_r, xa_s, xa_r, yl_s, yl_r, ya_s, ya_r, xn_s, xn_r, xf_s, xf_r, yb_s, yb_r, xb_s, xb_r,
     zb_s, zb_r, core_s, core_r,
 ):
     seq, res = lax.axis_index("seq"), lax.axis_index("res")
@@ -57,6 +57,8 @@
     z_hi, y, core = lax.div(res, 16), lax.rem(lax.div(res, 2), 8), lax.rem(res, 2)
     z = z_hi * 4 + z_lo
 
+    z_slots = (0, 1, 3, 5, 7, 6, 4, 2)
+
     def along_x(k):
         return lax.rem(x + k, NX)
 
@@ -72,22 +74,22 @@
     z_peer = {k: device_at(x, y, along_z(k), core) for k in range(1, NZ)}
     far_first = (4, 3, 5, 2, 6, 1, 7)
 
+    pairs = (
+        (align_hbm, align), (gain_hbm, gain), (shift_hbm, shift), (wl_hbm, wl), (bl_hbm, bl),
+        (wr_hbm, wr), (br_hbm, br), (ow_hbm, ow), (ob_hbm, ob),
+    )
+    loads = [pltpu.make_async_copy(a, b, load_sems.at[n]) for n, (a, b) in enumerate(pairs)]
+    for load in loads:
+        load.start()
+
     barrier = pltpu.get_barrier_semaphore()
     everyone = [z_peer[k] for k in far_first] + [y_peer[k] for k in far_first]
     everyone += [x_peer[k] for k in (2, 1, 3)] + [sibling]
     for device in everyone:
         pl.semaphore_signal(barrier, inc=1, device_id=device, device_id_type=MESH)
 
-    pairs = (
-        (align_hbm, align), (gain_hbm, gain), (shift_hbm, shift), (wl_hbm, wl), (bl_hbm, bl),
-        (wr_hbm, wr), (br_hbm, br), (ow_hbm, ow), (ob_hbm, ob),
-    )
-    loads = [pltpu.make_async_copy(a, b, load_sems.at[n]) for n, (a, b) in enumerate(pairs)]
-    for load in loads:
-        load.start()
-    for load in loads:
+    for load in loads[:7]:
         load.wait()
-
     values = align[...].astype(F32).reshape(512, 256)
     centre = jnp.mean(values, axis=-1, keepdims=True)
     spread = jnp.mean((values - centre) ** 2, axis=-1, keepdims=True)
@@ -119,28 +121,60 @@
 
     pl.semaphore_wait(barrier, len(everyone))
 
-    def to_all(peers, order, sems, src, dst):
+    def to_all(axis, sems, src, dst):
         copies = []
-        for k in order:
-            copy = remote(src(k), dst, sems, k - 1, peers[k])
+        me, count, order, peer = axis
+        for n in range(count - 1):
+            place = order(n)
+            k = lax.rem(place - me + count, count)
+            copy = remote(
+                src(place), dst(place) if callable(dst) else dst, sems, k - 1, peer(place)
+            )
             copy.start()
             copies.append(copy)
         return copies
 
+    def rising(me):
+        return lambda n: n + jnp.where(n >= me, 1, 0)
+
+    on_z = z, NZ, rising(z), lambda place: device_at(x, y, place, core)
+    on_y = y, NY, rising(y), lambda place: device_at(x, place, z, core)
+    on_x = x, NX, lambda n: lax.rem(x + (2, 1, 3)[n], NX), lambda place: device_at(place, y, z, core)
+
     def arrive(copies):
         for copy in copies:
             copy.wait_recv()
 
-    x_order = (2, 1, 3)
-    za = to_all(z_peer, far_first, (za_s, za_r), lambda k: ra_first.at[lax.rem(along_z(k), 4)], ra_z.at[z])
-    yl = to_all(y_peer, far_first, (yl_s, yl_r), lambda k: l_first.at[along_y(k)], l_y.at[y])
-    yb = to_all(y_peer, far_first, (yb_s, yb_r), lambda k: rb_first, rb_y.at[y])
+    yl = to_all(on_y, (yl_s, yl_r), lambda to: l_first.at[to], l_y.at[y])
+    za = to_all(on_z, (za_s, za_r), lambda to: ra_first.at[lax.rem(to, 4)], ra_z.at[z])
+    yb = to_all(on_y, (yb_s, yb_r), lambda to: rb_first, rb_y.at[y])
+
+    def slot(dz):
+        return jnp.where(dz == 0, 0, jnp.where(dz <= 4, 2 * dz - 1, 2 * (8 - dz)))
 
     o, n = iota((128, 128), 0), iota((128, 128), 1)
     o_v, o_m, o_s = jnp.right_shift(o, 4), jnp.bitwise_and(jnp.right_shift(o, 1), 7), jnp.bitwise_and(o, 1)
     regroup = one_hot(n == o_m * 16 + o_v * 2 + o_s)
     o, n = iota((512, 512), 0), iota((512, 512), 1)
     turn = one_hot(n == jnp.bitwise_and(o, 15) * 32 + jnp.right_shift(o, 4))
+
+    arrive(yl)
+    moved = matmul(regroup, l_y[...].reshape(128, 128)).astype(BF16)
+    for v in range(2):
+        for h in range(4):
+            l_by_z[v, :, h * 128 : (h + 1) * 128] = moved[v * 64 + h * 16 : v * 64 + h * 16 + 16]
+    l_all[x, 0] = l_by_z[z_hi]
+
+    def to_z(steps, sems):
+        copies = []
+        for n, k in enumerate(steps):
+            src = l_by_z.at[lax.div(along_z(k), 4)]
+            copies.append(remote(src, l_all.at[x, z_slots[8 - k]], sems, n, z_peer[k]))
+            copies[-1].start()
+        return copies
+
+    near = to_z((2, 6, 1, 7), (near_s, near_r))
+    far = to_z((4, 3, 5), (far_s, far_r))
 
     arrive(za)
     moved = matmul(regroup, ra_z[...].reshape(128, 128)).astype(BF16)
@@ -148,15 +182,7 @@
         for h in range(2):
             ra_by_x[v, :, h * 128 : (h + 1) * 128] = moved[v * 32 + h * 16 : v * 32 + h * 16 + 16]
     ra_all[y, x] = ra_by_x[x]
-    xa = to_all(x_peer, x_order, (xa_s, xa_r), lambda k: ra_by_x.at[along_x(k)], ra_all.at[y, x])
-
-    arrive(yl)
-    moved = matmul(regroup, l_y[...].reshape(128, 128)).astype(BF16)
-    for v in range(2):
-        for h in range(4):
-            l_by_z[v, :, h * 128 : (h + 1) * 128] = moved[v * 64 + h * 16 : v * 64 + h * 16 + 16]
-    l_z[z] = l_by_z[z_hi]
-    zl = to_all(z_peer, far_first, (zl_s, zl_r), lambda k: l_by_z.at[lax.div(along_z(k), 4)], l_z.at[z])
+    xa = to_all(on_x, (xa_s, xa_r), lambda to: ra_by_x.at[to], ra_all.at[y, x])
 
     arrive(yb)
     wide = jnp.concatenate(
@@ -170,24 +196,33 @@
                     v * 32 + h * 16 : v * 32 + h * 16 + 16, a * 128 : (a + 1) * 128
                 ]
     rb_x[:, x] = rb_by_x[x]
-    xb = to_all(x_peer, x_order, (xb_s, xb_r), lambda k: rb_by_x.at[along_x(k)], rb_x.at[:, x])
+    xb = to_all(on_x, (xb_s, xb_r), lambda to: rb_by_x.at[to], rb_x.at[:, x])
 
     arrive(xa)
-    ya = to_all(y_peer, far_first, (ya_s, ya_r), lambda k: ra_all.at[y], ra_all.at[y])
+    ya = to_all(on_y, (ya_s, ya_r), lambda to: ra_all.at[y], ra_all.at[y])
 
     arrive(xb)
-    rb_all[z] = rb_x[z_lo]
-    zb = to_all(z_peer, far_first, (zb_s, zb_r), lambda k: rb_x.at[lax.rem(along_z(k), 4)], rb_all.at[z])
-
-    arrive(zl)
-    l_t[x] = lax.dot_general(
-        turn, l_z[...].reshape(128, 512), (((1,), (1,)), ((), ())), preferred_element_type=F32
-    ).astype(BF16)
-    xl = to_all(x_peer, x_order, (xl_s, xl_r), lambda k: l_t.at[x], l_t.at[x])
-
+    rb_all[0] = rb_x[z_lo]
+    zb = to_all(
+        on_z, (zb_s, zb_r), lambda to: rb_x.at[lax.rem(to, 4)],
+        lambda to: rb_all.at[slot(lax.rem(z - to + NZ, NZ))],
+    )
+
+    arrive(near)
+    xn = to_all(on_x, (xn_s, xn_r), lambda to: l_all.at[x, pl.ds(0, 5)], l_all.at[x, pl.ds(0, 5)])
+
+    arrive(far)
+    xf = to_all(on_x, (xf_s, xf_r), lambda to: l_all.at[x, pl.ds(5, 3)], l_all.at[x, pl.ds(5, 3)])
+
+    o, n = iota((128, 128), 0), iota((128, 128), 1)
+    o_slot = jnp.right_shift(o, 4)
+    o_half = jnp.right_shift(o_slot + 1, 1)
+    o_z = jnp.bitwise_and(z + jnp.where(jnp.bitwise_and(o_slot, 1) == 1, o_half, 8 - o_half), 7)
+    o_y = jnp.bitwise_and(jnp.right_shift(o, 1), 7)
+    by_slot = one_hot(n == o_y * 16 + o_z * 2 + jnp.bitwise_and(o, 1))
     arrive(ya)
     right_a = [
-        matmul(regroup, jnp.concatenate([ra_all[b, a] for b in range(NY)], axis=0)).astype(BF16)
+        matmul(by_slot, jnp.concatenate([ra_all[b, a] for b in range(NY)], axis=0)).astype(BF16)
         for a in range(NX)
     ]
     arrive(zb)
@@ -195,25 +230,28 @@
     right = jnp.concatenate(
         [jnp.concatenate(right_a, axis=0), jnp.concatenate(right_b, axis=0)], axis=1
     )
-    arrive(xl)
-    left = jnp.concatenate([l_t[a] for a in range(NX)], axis=1)
+    arrive(xn + xf)
+    left = lax.dot_general(
+        turn, l_all[...].reshape(512, 512), (((1,), (1,)), ((), ())), preferred_element_type=F32
+    ).astype(BF16)
     outer = (matmul(left, right) * (1.0 / 1024)).astype(BF16)
     lane = iota((128, 128), 1)
     low, even = lane < 64, jnp.bitwise_and(lane, 32) == 0
     blocks = outer.reshape(8, 4, 16, 512)
     for h in range(4):
         a, b, c, d = (
-            blocks[:, n, :, h * 128 : (h + 1) * 128].reshape(128, 128).astype(F32) for n in range(4)
+            blocks[:, n, :, h * 128 : (h + 1) * 128].reshape(128, 128) for n in range(4)
         )
         a, c = jnp.where(low, a, pltpu.roll(c, 64, 1)), jnp.where(low, pltpu.roll(a, 64, 1), c)
         b, d = jnp.where(low, b, pltpu.roll(d, 64, 1)), jnp.where(low, pltpu.roll(b, 64, 1), d)
         a, b = jnp.where(even, a, pltpu.roll(b, 32, 1)), jnp.where(even, pltpu.roll(a, 96, 1), b)
         c, d = jnp.where(even, c, pltpu.roll(d, 32, 1)), jnp.where(even, pltpu.roll(c, 96, 1), d)
         for n, block in enumerate((a, b, c, d)):
-            block = block.astype(BF16)
             row = (h * 4 + n) * 16
             for m in range(8):
                 t_ref[row : row + 16, m * 128 : (m + 1) * 128] = block[m * 16 : m * 16 + 16]
+    for load in loads[7:]:
+        load.wait()
     term = matmul(t_ref[...], ow[...]).reshape(16, 2, 8, 128)
     half_out[...] = jnp.where(core == 0, term[:, 1], term[:, 0]).reshape(128, 128)
     swap = remote(half_out, half_in, (core_s, core_r), 0, sibling)
@@ -223,7 +261,7 @@
     total[...] = kept + half_in[...]
     for i in range(8):
         out_ref[i] = (total[pl.ds(i, 16, stride=8), :] + ob[...]).astype(BF16)
-    for copy in za + yl + yb + xa + zl + xb + ya + zb + xl + [swap]:
+    for copy in za + yl + yb + xa + near + far + xn + xf + xb + ya + zb + [swap]:
         copy.wait_send()
 
 
@@ -245,18 +283,17 @@
         pltpu.VMEM((2, 16, 512), BF16),
         pltpu.VMEM((4, 16, 256), BF16),
         pltpu.VMEM((4, 4, 16, 256), BF16),
-        pltpu.VMEM((8, 16, 512), BF16),
+        pltpu.VMEM((4, 8, 16, 512), BF16),
         pltpu.VMEM((8, 4, 16, 256), BF16),
         pltpu.VMEM((4, 4, 16, 256), BF16),
         pltpu.VMEM((8, 4, 16, 256), BF16),
-        pltpu.VMEM((4, 512, 128), BF16),
         pltpu.VMEM((256, 1024), BF16),
         pltpu.VMEM((128, 128), F32),
         pltpu.VMEM((128, 128), F32),
         pltpu.VMEM((128, 128), F32),
         dma((len(args),)),
     ]
-    for n in (7, 7, 3, 7, 7, 3, 7, 3, 7, 1):
+    for n in (7, 4, 3, 3, 7, 7, 3, 3, 7, 3, 7, 1):
         scratch += [dma((n,)), dma((n,))]
     args = tuple(pltpu.with_memory_space_constraint(a, pltpu.HBM) for a in args)
     return pl.pallas_call(

time: 36.1 us -> 34.8 us (0.964)
  Pallas kernels: 35.3 us -> 34 us
    pallas_call x1, Pallas kernels: 35.3 us -> 34 us  [body(): pl.pallas_call(kernel, out_shape=jax.ShapeDtypeStruct((8, 16, 128), BF16)...]
where the time goes in v4:
time: 34.8 us; the launch traced here: 34.6 us
  Pallas kernels  34 us (98%)
  local copies, waits for them, and re-layouts  0.62 us (2%)
    pallas_call x1, Pallas kernels, body(): pl.pallas_call(kernel, out_shape=jax.ShapeDtypeStruct((8, 16, 128), BF16)...  34 us

profile of v4, /device:TPU:1, one launch (start us, length us, event | category | flops | bytes accessed | tf_op | source)
XLA Modules:
  0.0 34.6 jit_solution(9268431185346119067)
XLA Ops:
  0.0 34.0 %shard_map.91 = bf16[8,16,128]{2,1,0:T(8,128)(2,1)S(1)} custom-call(bf16[2,256,256]{2,1,0:T(8,128)(2,1)} %align_hbm.1, f32[1,256]{1,0:T(1,128)} %bitcast.9, f32[1,256]{1,0:T(1,128)} %bitcast.10, bf16[32,256]{1,0:T(8,128)(2,1)} %bitcast.7, f32[1,32]{1,0:T(1,128)} %bitcast.11, bf16[32,256]{1,0:T(8,128)(2,1)} %bitcast.8, f32[1,32]{1,0:T(1,128)} %bitcast.12, ...), custom_call_target="tpu_custom_call" | custom-call | tf_op jit(solution)/shard_map/pallas_call | solution.py:299
  34.0 0.6 %copy.11 = bf16[8,16,128]{2,1,0:T(8,128)(2,1)} copy(bf16[8,16,128]{2,1,0:T(8,128)(2,1)S(1)} %shard_map.91) | data formatting | bytes 65536

commit v5 on v4

--- a/solution.py
+++ b/solution.py
@@ -13,6 +13,14 @@
 NX, NY, NZ = 4, 8, 8
 
 
+def low_bits(n, size):
+    return jnp.bitwise_and(n, size - 1)
+
+
+def high_bits(n, size):
+    return jnp.right_shift(n, size.bit_length() - 1)
+
+
 def iota(shape, dim):
     return lax.broadcasted_iota(jnp.int32, shape, dim)
 
@@ -30,7 +38,7 @@
 
 
 def device_at(x, y, z, core):
-    return (x * 4 + lax.rem(z, 4), lax.div(z, 4) * 16 + y * 2 + core)
+    return (x * 4 + low_bits(z, 4), high_bits(z, 4) * 16 + y * 2 + core)
 
 
 def remote(src, dst, sems, k, device):
@@ -53,20 +61,20 @@
     zb_s, zb_r, core_s, core_r,
 ):
     seq, res = lax.axis_index("seq"), lax.axis_index("res")
-    x, z_lo = lax.div(seq, 4), lax.rem(seq, 4)
-    z_hi, y, core = lax.div(res, 16), lax.rem(lax.div(res, 2), 8), lax.rem(res, 2)
+    x, z_lo = high_bits(seq, 4), low_bits(seq, 4)
+    z_hi, y, core = high_bits(res, 16), low_bits(high_bits(res, 2), 8), low_bits(res, 2)
     z = z_hi * 4 + z_lo
 
     z_slots = (0, 1, 3, 5, 7, 6, 4, 2)
 
     def along_x(k):
-        return lax.rem(x + k, NX)
+        return low_bits(x + k, NX)
 
     def along_y(k):
-        return lax.rem(y + k, NY)
+        return low_bits(y + k, NY)
 
     def along_z(k):
-        return lax.rem(z + k, NZ)
+        return low_bits(z + k, NZ)
 
     sibling = device_at(x, y, z, 1 - core)
     x_peer = {k: device_at(along_x(k), y, z, core) for k in range(1, NX)}
@@ -88,21 +96,6 @@
     for device in everyone:
         pl.semaphore_signal(barrier, inc=1, device_id=device, device_id_type=MESH)
 
-    for load in loads[:7]:
-        load.wait()
-    values = align[...].astype(F32).reshape(512, 256)
-    centre = jnp.mean(values, axis=-1, keepdims=True)
-    spread = jnp.mean((values - centre) ** 2, axis=-1, keepdims=True)
-    normed = ((values - centre) * lax.rsqrt(spread + 1e-05) * gain[...] + shift[...]).astype(BF16)
-    repeat = one_hot(jnp.bitwise_and(iota((32, 128), 1), 31) == iota((32, 128), 0))
-    weights = jnp.concatenate(
-        [contract_rows(w[...], repeat).astype(BF16) for w in (wl, wr)], axis=1
-    )
-    biases = jnp.concatenate([bl[...]] * 4 + [br[...]] * 4, axis=1)
-    projected = matmul(normed, weights) + biases
-    lane_group = jnp.bitwise_and(jnp.right_shift(iota((512, 256), 1), 5), 3)
-    mine = jnp.bitwise_and(iota((512, 256), 0), 3) == lane_group
-    spaced = jnp.where(mine, projected, 0.0).astype(BF16)
     o, n = iota((128, 512), 0), iota((128, 512), 1)
     n_s, n_h = jnp.right_shift(n, 8), jnp.bitwise_and(jnp.right_shift(n, 2), 3)
     n_y, n_zh = jnp.bitwise_and(jnp.right_shift(n, 4), 7), jnp.bitwise_and(jnp.right_shift(n, 7), 1)
@@ -111,6 +104,22 @@
     row_a = n_zl * 16 + n_x * 4 + n_h * 2 + n_s
     row_b = 64 + n_x * 16 + n_zl * 4 + (n_h - 2) * 2 + n_s
     pick_r = one_hot(o == jnp.where(n_h < 2, row_a, row_b))
+    repeat = one_hot(jnp.bitwise_and(iota((32, 128), 1), 31) == iota((32, 128), 0))
+    for load in loads[1:7]:
+        load.wait()
+    weights = jnp.concatenate(
+        [contract_rows(w[...], repeat).astype(BF16) for w in (wl, wr)], axis=1
+    )
+    biases = jnp.concatenate([bl[...]] * 4 + [br[...]] * 4, axis=1)
+    loads[0].wait()
+    values = align[...].astype(F32).reshape(512, 256)
+    centre = jnp.mean(values, axis=-1, keepdims=True)
+    spread = jnp.mean((values - centre) ** 2, axis=-1, keepdims=True)
+    normed = ((values - centre) * lax.rsqrt(spread + 1e-05) * gain[...] + shift[...]).astype(BF16)
+    projected = matmul(normed, weights) + biases
+    lane_group = jnp.bitwise_and(jnp.right_shift(iota((512, 256), 1), 5), 3)
+    mine = jnp.bitwise_and(iota((512, 256), 0), 3) == lane_group
+    spaced = jnp.where(mine, projected, 0.0).astype(BF16)
     l_first[...] = matmul(pick_l, spaced[:, :128]).astype(BF16).reshape(8, 16, 128)
     picked = matmul(pick_r, spaced[:, 128:]).astype(BF16)
     ra_first[...] = picked[:64].reshape(4, 16, 128)
@@ -126,7 +135,7 @@
         me, count, order, peer = axis
         for n in range(count - 1):
             place = order(n)
-            k = lax.rem(place - me + count, count)
+            k = low_bits(place - me + count, count)
             copy = remote(
                 src(place), dst(place) if callable(dst) else dst, sems, k - 1, peer(place)
             )
@@ -139,14 +148,14 @@
 
     on_z = z, NZ, rising(z), lambda place: device_at(x, y, place, core)
     on_y = y, NY, rising(y), lambda place: device_at(x, place, z, core)
-    on_x = x, NX, lambda n: lax.rem(x + (2, 1, 3)[n], NX), lambda place: device_at(place, y, z, core)
+    on_x = x, NX, lambda n: low_bits(x + (2, 1, 3)[n], NX), lambda place: device_at(place, y, z, core)
 
     def arrive(copies):
         for copy in copies:
             copy.wait_recv()
 
     yl = to_all(on_y, (yl_s, yl_r), lambda to: l_first.at[to], l_y.at[y])
-    za = to_all(on_z, (za_s, za_r), lambda to: ra_first.at[lax.rem(to, 4)], ra_z.at[z])
+    za = to_all(on_z, (za_s, za_r), lambda to: ra_first.at[low_bits(to, 4)], ra_z.at[z])
     yb = to_all(on_y, (yb_s, yb_r), lambda to: rb_first, rb_y.at[y])
 
     def slot(dz):
@@ -168,7 +177,7 @@
     def to_z(steps, sems):
         copies = []
         for n, k in enumerate(steps):
-            src = l_by_z.at[lax.div(along_z(k), 4)]
+            src = l_by_z.at[high_bits(along_z(k), 4)]
             copies.append(remote(src, l_all.at[x, z_slots[8 - k]], sems, n, z_peer[k]))
             copies[-1].start()
         return copies
@@ -204,8 +213,8 @@
     arrive(xb)
     rb_all[0] = rb_x[z_lo]
     zb = to_all(
-        on_z, (zb_s, zb_r), lambda to: rb_x.at[lax.rem(to, 4)],
-        lambda to: rb_all.at[slot(lax.rem(z - to + NZ, NZ))],
+        on_z, (zb_s, zb_r), lambda to: rb_x.at[low_bits(to, 4)],
+        lambda to: rb_all.at[slot(low_bits(z - to + NZ, NZ))],
     )
 
     arrive(near)
@@ -257,12 +266,13 @@
     swap = remote(half_out, half_in, (core_s, core_r), 0, sibling)
     swap.start()
     kept = jnp.where(core == 0, term[:, 0], term[:, 1]).reshape(128, 128)
+    for copy in za + yl + yb + xa + near + far + xn + xf + xb + ya + zb:
+        copy.wait_send()
     arrive([swap])
     total[...] = kept + half_in[...]
     for i in range(8):
         out_ref[i] = (total[pl.ds(i, 16, stride=8), :] + ob[...]).astype(BF16)
-    for copy in za + yl + yb + xa + near + far + xn + xf + xb + ya + zb + [swap]:
-        copy.wait_send()
+    swap.wait_send()
 
 
 def body(alignment, gain, shift, wl, bl, wr, br, ow, ob):

time: 34.8 us -> 34.7 us (level)
  no operation moved by 1% of the time
where the time goes in v5:
time: 34.7 us; the launch traced here: 34.5 us
  Pallas kernels  33.9 us (98%)
  local copies, waits for them, and re-layouts  0.62 us (2%)
    pallas_call x1, Pallas kernels, body(): pl.pallas_call(kernel, out_shape=jax.ShapeDtypeStruct((8, 16, 128), BF16)...  33.9 us

profile of v5, /device:TPU:1, one launch (start us, length us, event | category | flops | bytes accessed | tf_op | source)
XLA Modules:
  0.0 34.5 jit_solution(14308619316344911350)
XLA Ops:
  0.0 33.9 %shard_map.91 = bf16[8,16,128]{2,1,0:T(8,128)(2,1)S(1)} custom-call(bf16[2,256,256]{2,1,0:T(8,128)(2,1)} %align_hbm.1, f32[1,256]{1,0:T(1,128)} %bitcast.9, f32[1,256]{1,0:T(1,128)} %bitcast.10, bf16[32,256]{1,0:T(8,128)(2,1)} %bitcast.7, f32[1,32]{1,0:T(1,128)} %bitcast.11, bf16[32,256]{1,0:T(8,128)(2,1)} %bitcast.8, f32[1,32]{1,0:T(1,128)} %bitcast.12, ...), custom_call_target="tpu_custom_call" | custom-call | tf_op jit(solution)/shard_map/pallas_call | solution.py:309
  33.9 0.6 %copy.11 = bf16[8,16,128]{2,1,0:T(8,128)(2,1)} copy(bf16[8,16,128]{2,1,0:T(8,128)(2,1)S(1)} %shard_map.91) | data formatting | bytes 65536

commit v6 on v5

--- a/solution.py
+++ b/solution.py
@@ -182,8 +182,8 @@
             copies[-1].start()
         return copies
 
+    far = to_z((4, 3, 5), (far_s, far_r))
     near = to_z((2, 6, 1, 7), (near_s, near_r))
-    far = to_z((4, 3, 5), (far_s, far_r))
 
     arrive(za)
     moved = matmul(regroup, ra_z[...].reshape(128, 128)).astype(BF16)

time: 34.7 us -> 34.5 us (level)
  no operation moved by 1% of the time
where the time goes in v6:
time: 34.5 us; the launch traced here: 34.4 us
  Pallas kernels  33.8 us (98%)
  local copies, waits for them, and re-layouts  0.62 us (2%)
    pallas_call x1, Pallas kernels, body(): pl.pallas_call(kernel, out_shape=jax.ShapeDtypeStruct((8, 16, 128), BF16)...  33.8 us

profile of v6, /device:TPU:1, one launch (start us, length us, event | category | flops | bytes accessed | tf_op | source)
XLA Modules:
  0.0 34.4 jit_solution(1313073878669582097)
XLA Ops:
  0.0 33.8 %shard_map.91 = bf16[8,16,128]{2,1,0:T(8,128)(2,1)S(1)} custom-call(bf16[2,256,256]{2,1,0:T(8,128)(2,1)} %align_hbm.1, f32[1,256]{1,0:T(1,128)} %bitcast.9, f32[1,256]{1,0:T(1,128)} %bitcast.10, bf16[32,256]{1,0:T(8,128)(2,1)} %bitcast.7, f32[1,32]{1,0:T(1,128)} %bitcast.11, bf16[32,256]{1,0:T(8,128)(2,1)} %bitcast.8, f32[1,32]{1,0:T(1,128)} %bitcast.12, ...), custom_call_target="tpu_custom_call" | custom-call | tf_op jit(solution)/shard_map/pallas_call | solution.py:309
  33.8 0.6 %copy.11 = bf16[8,16,128]{2,1,0:T(8,128)(2,1)} copy(bf16[8,16,128]{2,1,0:T(8,128)(2,1)S(1)} %shard_map.91) | data formatting | bytes 65536
